TPU v7x, 32 devices: a whole 2x2x4 slice. The times are simulated.
32 devices in a mesh: site: 2 (over y), pt: 4 (over z), var: 2 (over x), cmp: 2 (over core).
Axes of the slice: x: 2, y: 2, z: 4, core: 2. Of those that a mesh axis runs over, the one named last changes fastest.
Arguments:
- strain_green: bfloat16 [5120, 24, 256], P(('site', 'pt'), None, 'cmp'), parts along dimension 0, may hold values from -2.390625 to 2.390625
- green_scale: float32 [40, 24], P(('site', 'pt')), parts along dimension 0, may hold values from 0.3 to 3
- mechanism: float32 [6, 2560], P(None, 'pt'), may hold values from -4 to 4
- slip_amplitude: bfloat16 [4, 32, 1536], P('pt', 'var'), may hold values from 0.19921875 to 2
- onset_time: float32 [4, 32, 1536], P('pt', 'var'), may hold values from 0 to 128
- rupture_row: int32 [4], replicated, may hold values from 0 to 3, each once
- rupture_blocks: int32 [4, 12], replicated, may hold values from 0 to 19, as said below
- block_count: int32 [4], replicated, may hold values from 1 to 12, 16 in all
- crossover: int32 [4], replicated, may hold values from 128 to 251
- high_band: float32 [8, 32, 2, 512], P(('site', 'pt'), 'var', None, 'cmp'), parts along dimension 0, may hold values from -6 to 6
Outputs:
- seismograms: float32 [8, 32, 2, 512], P(('site', 'pt'), 'var', None, 'cmp'), parts along dimension 0
There are 2 independent parts, one for each index of `site`. A program takes and returns all parts, laid end to end along the dimension named above; an argument that names none is the same for every part. Nothing has to cross between parts.
Inputs may be any that keep to these rules, and one draw needn't show every extreme that they name: `rupture_blocks`: each row names 12 different point blocks; rupture r covers the first block_count[r] of them.
All inputs are finite; a program needn't handle non-finite values.
Results may differ from a plain program's by a relative error of at most 0.0028.
Values may be sent and summed in bfloat16 or wider, within the bound.
No kernel may reach another device: no remote copies, remote signals or barrier semaphores. Data moves between devices by JAX's collectives and lax.ppermute only.
A program may use at most 64 MiB of HBM per device.

v0:
```python
import math

import jax
import jax.numpy as jnp
from jax import lax
from jax.sharding import PartitionSpec as P

taper_width = 8.0


def green_tensor(strain_green, green_scale, mechanism):
    points = strain_green.shape[0]
    bins_here = strain_green.shape[2]
    blocks_scale = jnp.repeat(green_scale, points // green_scale.shape[0], axis=0)
    factors = blocks_scale.reshape(points, 4, 6) * jnp.transpose(mechanism)[:, None, :]
    spectra = strain_green.reshape(points, 4, 6, bins_here).astype(jnp.float32)
    summed = jnp.einsum("pkjf,pkj->pkf", spectra, factors, precision=lax.Precision.HIGHEST)
    return summed.astype(jnp.bfloat16)


def block_term(green_block, amplitude, onset_block, phase_step):
    angles = onset_block[:, :, None] * phase_step[None, None, :]
    weight = amplitude.astype(jnp.float32)[:, :, None]
    with_cos = weight * jnp.cos(angles)
    with_sin = weight * jnp.sin(angles)
    real_list = []
    imag_list = []
    for component in range(2):
        real_green = green_block[:, component, :][None, :, :]
        imag_green = green_block[:, 2 + component, :][None, :, :]
        real_list.append(jnp.sum(with_cos * real_green + with_sin * imag_green, axis=1))
        imag_list.append(jnp.sum(with_cos * imag_green - with_sin * real_green, axis=1))
    return jnp.stack(real_list + imag_list, axis=1)


def live_pairs(blocks, covered, lowest, beyond):
    slot_total = blocks.shape[1]
    slot_ids = jnp.arange(slot_total)[None, :]
    inside = (slot_ids < covered[:, None]) & (blocks >= lowest) & (blocks < beyond)
    live_flags = inside.reshape(-1).astype(jnp.int32)
    ordering = jnp.argsort(1 - live_flags, stable=True)
    return (ordering, jnp.sum(live_flags))


def accumulate(
    running,
    ordering,
    number_live,
    slot_total,
    fetch_green,
    amplitudes,
    onsets,
    phase_step,
    block_points,
):

    def visit(counter, running):
        pair_number = ordering[counter]
        row_number = pair_number // slot_total
        slot_number = pair_number % slot_total
        green_block = fetch_green(row_number, slot_number)
        offset = slot_number * block_points
        amplitude = lax.dynamic_slice_in_dim(amplitudes[row_number], offset, block_points, 1)
        onset_block = lax.dynamic_slice_in_dim(onsets[row_number], offset, block_points, 1)
        contribution = block_term(green_block, amplitude, onset_block, phase_step)
        current = lax.dynamic_index_in_dim(running, row_number, 0, keepdims=False)
        return lax.dynamic_update_index_in_dim(running, current + contribution, row_number, 0)

    return lax.fori_loop(0, number_live, visit, running)


def body(
    strain_green,
    green_scale,
    mechanism,
    slip_amplitude,
    onset_time,
    rupture_row,
    rupture_blocks,
    block_count,
    crossover,
    high_band,
):
    highest = lax.Precision.HIGHEST
    points_here = strain_green.shape[0]
    bins_here = strain_green.shape[2]
    blocks_here = green_scale.shape[0]
    block_points = points_here // blocks_here
    rows_here = slip_amplitude.shape[0]
    variations = slip_amplitude.shape[1]
    slot_total = slip_amplitude.shape[2] // block_points
    bin_half = lax.axis_index("cmp")
    samples = 2 * bins_here * lax.axis_size("cmp")
    bins_global = bin_half * bins_here + jnp.arange(bins_here)
    frequency = bins_global.astype(jnp.float32)
    phase_step = frequency * (2.0 * math.pi / samples)
    green_blocks = green_tensor(strain_green, green_scale, mechanism).reshape(
        blocks_here, block_points, 4, bins_here
    )
    first_row = lax.axis_index("pt") * rows_here
    own_ruptures = lax.dynamic_slice_in_dim(rupture_row, first_row, rows_here, 0)
    all_amplitudes, all_onsets = (
        lax.all_gather(slip_amplitude.astype(jnp.float32), "pt", axis=0, tiled=True).astype(
            slip_amplitude.dtype
        ),
        lax.all_gather(onset_time, "pt", axis=0, tiled=True),
    )
    lowest = lax.axis_index("pt") * blocks_here
    blocks = rupture_blocks[rupture_row]
    ordering, number_live = live_pairs(
        blocks, block_count[rupture_row], lowest, lowest + blocks_here
    )

    def fetch_green(row_number, slot_number):
        return lax.dynamic_index_in_dim(
            green_blocks, blocks[row_number, slot_number] - lowest, 0, keepdims=False
        )

    initial = jnp.zeros((rows_here * lax.axis_size("pt"), variations, 4, bins_here), jnp.float32)
    spectrum = lax.psum_scatter(
        accumulate(
            initial,
            ordering,
            number_live,
            slot_total,
            fetch_green,
            all_amplitudes,
            all_onsets,
            phase_step,
            block_points,
        ),
        "pt",
        scatter_dimension=0,
        tiled=True,
    )
    all_band = lax.all_gather(high_band, "cmp", axis=3, tiled=True)
    sample_ids = jnp.arange(samples)
    angles = (bins_global[:, None] * sample_ids[None, :] % samples).astype(jnp.float32) * (
        2.0 * math.pi / samples
    )
    cosine = jnp.cos(angles)
    sine_table = jnp.sin(angles)
    band_rows = all_band.reshape(-1, samples)
    band_real = jnp.dot(band_rows, cosine.T, precision=highest)
    band_imag = -jnp.dot(band_rows, sine_table.T, precision=highest)
    crossing = crossover[own_ruptures].astype(jnp.float32)
    taper_weight = jnp.clip((crossing[:, None] - frequency[None, :]) / taper_width + 0.5, 0.0, 1.0)
    taper_rows = jnp.repeat(taper_weight, variations * 2, axis=0)
    spectrum_real = spectrum[:, :, 0:2].reshape(-1, bins_here)
    spectrum_imag = spectrum[:, :, 2:4].reshape(-1, bins_here)
    coefficient = jnp.where(bins_global == 0, 1.0, 2.0) / samples
    excess_real = taper_rows * (spectrum_real - band_real) * coefficient
    excess_imag = taper_rows * (spectrum_imag - band_imag) * coefficient
    basis_table = jnp.concatenate([cosine, -sine_table], axis=0)
    partial_value = jnp.dot(
        jnp.concatenate([excess_real, excess_imag], axis=1), basis_table, precision=highest
    )
    partial_value = partial_value.reshape(rows_here, variations, 2, samples)
    low_band = lax.psum_scatter(partial_value, "cmp", scatter_dimension=3, tiled=True)
    return high_band + low_band


def solution(mesh):
    return jax.shard_map(
        body,
        mesh=mesh,
        in_specs=(
            P(("site", "pt"), None, "cmp"),
            P(("site", "pt"), None),
            P(None, "pt"),
            P("pt", "var", None),
            P("pt", "var", None),
            P(),
            P(),
            P(),
            P(),
            P(("site", "pt"), "var", None, "cmp"),
        ),
        out_specs=P(("site", "pt"), "var", None, "cmp"),
        check_vma=False,
    )
```

profile of v0, /device:TPU:0, one launch (start us, length us, event | category | flops | bytes accessed | tf_op | source)
XLA Modules:
  0.0 166.4 jit_solution(17201936582558625197)
XLA Ops:
  7.8 1.3 gather_fusion
  9.9 4.9 %copy.24 = bf16[640,24,128]{2,0,1:T(8,128)(2,1)} copy(bf16[640,24,128]{2,1,0:T(8,128)(2,1)} %param.12) | data formatting | bytes 7864320 | tf_op args[0]
  15.0 1.3 copy.28
  16.4 16.4 %fusion.25 = bf16[640,4,1,128]{3,2,1,0:T(2,128)(2,1)S(1)} fusion(f32[640,4,6,1]{2,3,1,0:T(1,128)S(1)} %copy.28, bf16[640,4,6,128]{3,0,2,1:T(8,128)(2,1)} %bitcast.100), kind=kOutput, calls=%fused_computation.37 | convolution fusion | flops 23592960 | bytes 4648960 | tf_op jit(solution)/shard_map/pkjf,pkj->pkf/dot_general | solution.py:17
  33.0 16.2 %all_gather.10 = f32[4,16,1536]{2,1,0:T(8,128)S(1)} all-gather(f32[1,16,1536]{2,1,0:T(8,128)S(1)} %copy-done.3), channel_id=1, replica_groups=mesh['site'=2,'pt'=4,'var'=2,'cmp'=2] {'pt'}, dimensions={0}, use_global_device_ids=true | all-gather | bytes 491520 | tf_op jit(solution)/shard_map/all_gather | solution.py:106
  49.2 14.3 %all_gather.9 = bf16[4,16,1536]{2,1,0:T(8,128)(2,1)S(1)} all-gather(bf16[1,16,1536]{2,1,0:T(8,128)(2,1)S(1)} %copy-done.4), channel_id=1, replica_groups=mesh['site'=2,'pt'=4,'var'=2,'cmp'=2] {'pt'}, dimensions={0}, use_global_device_ids=true | all-gather | bytes 245760 | tf_op jit(solution)/shard_map/all_gather | solution.py:103
  63.5 2.1 %sort.17 = (s32[48]{0:T(128)}, s32[48]{0:T(128)S(1)}) sort(s32[48]{0:T(128)S(1)} %reshape.190, s32[48]{0:T(128)S(1)} %iota.20), dimensions={0}, to_apply=%region_1.2 | sort | flops 288 | bytes 768 | tf_op jit(solution)/shard_map/jit(argsort)/sort | solution.py:41
  65.6 53.1 %while.15 = (s32[]{:T(128)}, f32[4,16,4,128]{3,1,2,0:T(8,128)S(1)}, s32[]{:T(128)}, s32[48]{0:T(128)S(1)}, bf16[4,16,1536]{2,1,0:T(8,128)(2,1)S(1)}, /*index=5*/...) while((s32[]{:T(128)}, f32[4,16,4,128]{3,1,2,0:T(8,128)S(1)}, ...), condition=%wide.region_7.8_spmd.clone, body=%wide.region_2.7_spmd.clone.sunk | while | flops 5073313 | bytes 1095254 | solution.py:69
  70.7 5.5 %fusion.73 = (f32[16,128]{1,0:T(8,128)S(1)}, f32[16,128]{1,0:T(8,128)S(1)}, f32[16,128]{1,0:T(8,128)S(1)}, f32[16,128]{1,0:T(8,128)S(1)}) fusion(f32[128,128]{1,0:T(8,128)S(1)} %get-tuple-element.330, f32[128,128]{1,0:T(8,128)S(1)} %get-tuple-element.331, f32[128]{0:T(128)S(1)} %convert_multiply_fusion.2, ...), kind=kLoop, calls=%fused_computation.11.clone.1 | loop fusion | flops 4972544 | bytes 311808 | tf_op jit(solution)/shard_map/while/body/reduce_sum | solution.py:31
  81.1 5.5 %fusion.73 = (f32[16,128]{1,0:T(8,128)S(1)}, f32[16,128]{1,0:T(8,128)S(1)}, f32[16,128]{1,0:T(8,128)S(1)}, f32[16,128]{1,0:T(8,128)S(1)}) fusion(f32[128,128]{1,0:T(8,128)S(1)} %get-tuple-element.330, f32[128,128]{1,0:T(8,128)S(1)} %get-tuple-element.331, f32[128]{0:T(128)S(1)} %convert_multiply_fusion.2, ...), kind=kLoop, calls=%fused_computation.11.clone.1 | loop fusion | flops 4972544 | bytes 311808 | tf_op jit(solution)/shard_map/while/body/reduce_sum | solution.py:31
  91.6 5.5 %fusion.73 = (f32[16,128]{1,0:T(8,128)S(1)}, f32[16,128]{1,0:T(8,128)S(1)}, f32[16,128]{1,0:T(8,128)S(1)}, f32[16,128]{1,0:T(8,128)S(1)}) fusion(f32[128,128]{1,0:T(8,128)S(1)} %get-tuple-element.330, f32[128,128]{1,0:T(8,128)S(1)} %get-tuple-element.331, f32[128]{0:T(128)S(1)} %convert_multiply_fusion.2, ...), kind=kLoop, calls=%fused_computation.11.clone.1 | loop fusion | flops 4972544 | bytes 311808 | tf_op jit(solution)/shard_map/while/body/reduce_sum | solution.py:31
  102.1 5.5 %fusion.73 = (f32[16,128]{1,0:T(8,128)S(1)}, f32[16,128]{1,0:T(8,128)S(1)}, f32[16,128]{1,0:T(8,128)S(1)}, f32[16,128]{1,0:T(8,128)S(1)}) fusion(f32[128,128]{1,0:T(8,128)S(1)} %get-tuple-element.330, f32[128,128]{1,0:T(8,128)S(1)} %get-tuple-element.331, f32[128]{0:T(128)S(1)} %convert_multiply_fusion.2, ...), kind=kLoop, calls=%fused_computation.11.clone.1 | loop fusion | flops 4972544 | bytes 311808 | tf_op jit(solution)/shard_map/while/body/reduce_sum | solution.py:31
  112.6 5.5 %fusion.73 = (f32[16,128]{1,0:T(8,128)S(1)}, f32[16,128]{1,0:T(8,128)S(1)}, f32[16,128]{1,0:T(8,128)S(1)}, f32[16,128]{1,0:T(8,128)S(1)}) fusion(f32[128,128]{1,0:T(8,128)S(1)} %get-tuple-element.330, f32[128,128]{1,0:T(8,128)S(1)} %get-tuple-element.331, f32[128]{0:T(128)S(1)} %convert_multiply_fusion.2, ...), kind=kLoop, calls=%fused_computation.11.clone.1 | loop fusion | flops 4972544 | bytes 311808 | tf_op jit(solution)/shard_map/while/body/reduce_sum | solution.py:31
  123.3 2.0 %all_gather.11 = f32[1,16,2,512]{3,2,1,0:T(2,128)S(1)} all-gather(f32[1,16,2,256]{3,2,1,0:T(2,128)S(1)} %copy-done.2), channel_id=1, replica_groups=mesh['site'=2,'pt'=4,'var'=2,'cmp'=2] {'cmp'}, dimensions={3}, use_global_device_ids=true | all-gather | bytes 98304 | tf_op jit(solution)/shard_map/all_gather | solution.py:136
  125.4 1.1 fusion.45
  126.5 11.5 %reduce-scatter.5.cloned.1.call-done = f32[1,16,4,128]{3,1,2,0:T(8,128)} async-done(((f32[4,16,4,128]{3,1,2,0:T(8,128)}), f32[1,16,4,128]{3,1,2,0:T(8,128)}) %reduce-scatter.5.cloned.1.call-update) | async-done | bytes 32784 | tf_op jit(solution)/shard_map/reduce_scatter | solution.py:120
  138.0 0.7 fusion.65
  138.8 1.4 fusion.32
  140.2 1.4 fusion.33
  142.0 3.4 %copy.31 = f32[1,16,2,512]{2,1,0,3:T(8,128)} copy(f32[1,16,2,512]{3,2,1,0:T(2,128)S(1)} %reshape.161) | data formatting | bytes 131072
  145.4 4.3 %reshape.216 = f32[512,32]{1,0:T(8,128)} reshape(f32[512,1,16,2]{3,2,1,0:T(8,128)} %bitcast.98) | data formatting | bytes 131072
  149.7 6.0 %reduce-scatter.7.cloned.1.call-done = f32[256,32]{1,0:T(8,128)} async-done(((f32[512,32]{1,0:T(8,128)}), f32[256,32]{1,0:T(8,128)}) %reduce-scatter.7.cloned.1.call-update) | async-done | bytes 32784
  155.7 2.1 %reshape.217 = f32[256,1,16,2]{3,2,1,0:T(8,128)S(1)} reshape(f32[256,32]{1,0:T(8,128)} %reduce-scatter.7.cloned.1.call-done) | data formatting | bytes 65536
  157.8 1.1 copy.32
  (85 shorter events, 13.3 us)
Async XLA Ops:
  6.5 0.7 copy-start
  6.5 131.5 %reduce-scatter.5.cloned.1.call-start = ((), (), s32[]{:S(2)}) async-start(), calls=%async_computation.2 | async-start | bytes 163840 | tf_op jit(solution)/shard_map/reduce_scatter | solution.py:120
  9.9 4.9 %copy-start.6 = (f32[5,24]{1,0:T(8,128)S(1)}, f32[5,24]{1,0:T(8,128)}, u32[]{:S(2)}) copy-start(f32[5,24]{1,0:T(8,128)} %param.13) | copy-start | bytes 1444
  9.9 5.1 %copy-start.5 = (f32[6,640]{1,0:T(8,128)S(1)}, f32[6,640]{1,0:T(8,128)}, u32[]{:S(2)}) copy-start(f32[6,640]{1,0:T(8,128)} %param.14) | copy-start | bytes 46084
  16.4 16.6 %copy-start.3 = (f32[1,16,1536]{2,1,0:T(8,128)S(1)}, f32[1,16,1536]{2,1,0:T(8,128)}, u32[]{:S(2)}) copy-start(f32[1,16,1536]{2,1,0:T(8,128)} %param.16) | copy-start | bytes 294916
  16.4 32.8 %copy-start.4 = (bf16[1,16,1536]{2,1,0:T(8,128)(2,1)S(1)}, bf16[1,16,1536]{2,1,0:T(8,128)(2,1)}, u32[]{:S(2)}) copy-start(bf16[1,16,1536]{2,1,0:T(8,128)(2,1)} %param.15) | copy-start | bytes 147460
  65.6 53.9 %copy-start.7 = (s32[4]{0:T(128)S(1)}, s32[4]{0:T(128)}, u32[]{:S(2)}) copy-start(s32[4]{0:T(128)} %param.17) | copy-start | bytes 52
  65.6 56.4 %copy-start.8 = (s32[4]{0:T(128)S(1)}, s32[4]{0:T(128)}, u32[]{:S(2)}) copy-start(s32[4]{0:T(128)} %param.20) | copy-start | bytes 52
  65.6 57.7 %copy-start.2 = (f32[1,16,2,256]{3,2,1,0:T(2,128)S(1)}, f32[1,16,2,256]{3,2,1,0:T(2,128)}, u32[]{:S(2)}) copy-start(f32[1,16,2,256]{3,2,1,0:T(2,128)} %param.21) | copy-start | bytes 98308
  118.7 0.6 copy-start.1
  119.4 36.3 %reduce-scatter.7.cloned.1.call-start = ((), (), s32[]{:S(2)}) async-start(), calls=%async_computation.3 | async-start | bytes 393216
Sparse Core Ops, SparseCore 0:
  119.5 18.4 reduce-scatter.4
  149.8 5.8 reduce-scatter.6
where the time goes:
time: 168 us; the launch traced here: 166 us
  other arithmetic  33.2 us (20%)
  blocking collectives  32.5 us (19%)
  local copies, waits for them, and re-layouts  29.3 us (17%)
  matrix products  19.6 us (12%)
  loops' own time  18.1 us (11%)
  waiting for transfers between devices  17.5 us (10%)
  between operations  16.2 us (10%)
    reduce_sum x5, other arithmetic, block_term(): jnp.sum(with_cos * real_green + with_sin * imag_green, axis=1)  27.3 us
    another operation x1, loops' own time, accumulate(): return lax.fori_loop(0, number_live, visit, running)  18.1 us
    unnamed x24, local copies, waits for them, and re-layouts  16.6 us
    dot_general x1, matrix products, green_tensor(): jnp.einsum('pkjf,pkj->pkf', spectra, factors, precision=lax.Precision.HIG...  16.4 us
    all_gather x1, blocking collectives, body(): lax.all_gather(onset_time, 'pt', axis=0, tiled=True)  16.2 us
    all_gather x1, blocking collectives, body(): lax.all_gather(slip_amplitude.astype(jnp.float32), 'pt', axis=0, tiled=True)  14.3 us
    reduce_scatter x1, waiting for transfers between devices, body(): lax.psum_scatter(accumulate(initial, ordering, number_live, slot_total, f...  11.5 us
    unnamed x3, waiting for transfers between devices  6.01 us
  transfers between devices with their start and end apart: 2, of which 2 were waited for; matrix products, arithmetic and copies ran while one was open for 1% of the time, Pallas kernels for 0%

commit v1 on v0

v1 whole, which is shorter than its diff:
```python
import functools
import math

import jax
import jax.numpy as jnp
import ml_dtypes
import numpy as np
from jax import lax
from jax.experimental import pallas as pl
from jax.experimental.pallas import tpu as pltpu
from jax.sharding import PartitionSpec as P

taper_width = 8.0
f32 = jnp.float32
bf16 = jnp.bfloat16
highest = lax.Precision.HIGHEST
vmem_bytes = 48 * 1024 * 1024
SMEM = pl.BlockSpec(memory_space=pltpu.SMEM)
VMEM = pl.BlockSpec(memory_space=pltpu.VMEM)


def params():
    return pltpu.CompilerParams(vmem_limit_bytes=vmem_bytes)


def cost(flops, nbytes):
    return pl.CostEstimate(flops=flops, bytes_accessed=nbytes, transcendentals=0)


def split_table(table):
    high = table.astype(ml_dtypes.bfloat16)
    low = (table - high.astype(np.float64)).astype(ml_dtypes.bfloat16)
    return high, low


def fourier_table(bins, samples, samples_here):
    product = (np.arange(bins)[:, None] * np.arange(samples_here)[None, :]) % samples
    angle = product * (2.0 * np.pi / samples)
    return np.concatenate([np.cos(angle), -np.sin(angle)], axis=0)


def pack_kernel(blocks_here, block_points, row_ref, blocks_ref, count_ref, slip_ref, onset_ref, *outs):
    me = lax.axis_index("pt")
    rupture = row_ref[me]

    def visit(slot, carry):
        block = blocks_ref[rupture, slot]
        owner = block // blocks_here
        local = block - owner * blocks_here
        offset = pl.multiple_of(slot * block_points, block_points)
        onset = onset_ref[0, :, pl.ds(offset, block_points)]
        first = onset.astype(bf16)
        second = (onset - first.astype(f32)).astype(bf16)
        slip = slip_ref[0, :, pl.ds(offset, block_points)]
        for step, out in enumerate(outs):

            @pl.when(owner == jnp.bitwise_xor(me, step))
            def _():
                out[local, 0] = first
                out[local, 1] = second
                out[local, 2] = slip

        return carry

    lax.fori_loop(0, count_ref[rupture], visit, 0)


def green_kernel(strain_ref, scale_ref, mechanism_ref, out_ref):
    block_points, bins = mechanism_ref.shape[1], strain_ref.shape[1]
    rows = 24
    octet = 8
    wide = octet * rows
    column = lax.broadcasted_iota(jnp.int32, (6, wide), 1) % rows
    spread_six = (column % 6 == lax.broadcasted_iota(jnp.int32, (6, wide), 0)).astype(f32)
    column = lax.broadcasted_iota(jnp.int32, (rows, wide), 1) % rows
    spread_rows = (column == lax.broadcasted_iota(jnp.int32, (rows, wide), 0)).astype(f32)
    moments = lax.dot_general(
        mechanism_ref[...], spread_six, (((0,), (0,)), ((), ())), precision=highest,
        preferred_element_type=f32,
    )
    scales = jnp.dot(scale_ref[0], spread_rows, precision=highest, preferred_element_type=f32)
    factor = moments * scales
    column = lax.broadcasted_iota(jnp.int32, (octet, wide), 1)
    same_point = column // rows == lax.broadcasted_iota(jnp.int32, (octet, wide), 0)
    part = (column % rows) // 6
    masks = [same_point & (part == k) for k in range(4)]
    lane = lax.broadcasted_iota(jnp.int32, (2 * octet, bins), 1) % 4
    lanes = [lane == k for k in range(4)]
    low_lane = lane < 2
    for pair in range(block_points // (2 * octet)):
        spectra = [[], [], [], []]
        for half in range(2):
            first = pair * 2 * octet + half * octet
            here = factor[first : first + octet]
            coarse = here.astype(bf16).astype(f32)
            fine = here - coarse
            left = jnp.concatenate(
                [jnp.where(mask, coarse, 0.0) for mask in masks]
                + [jnp.where(mask, fine, 0.0) for mask in masks],
                axis=0,
            ).astype(bf16)
            strain = strain_ref[first * rows : first * rows + wide, :]
            both = jnp.dot(left, strain, preferred_element_type=f32)
            for k in range(4):
                spectra[k].append(
                    both[k * octet : (k + 1) * octet]
                    + both[(k + 4) * octet : (k + 5) * octet]
                )
        green = [jnp.concatenate(s, axis=0).astype(bf16).astype(f32) for s in spectra]
        place = pl.ds(pair * 2 * octet, 2 * octet)
        below = pl.ds(block_points + pair * 2 * octet, 2 * octet)
        for r in range(4):
            top = jnp.zeros_like(green[0])
            for k in range(4):
                moved = green[k] if k == r else pltpu.roll(green[k], (k - r) % bins, 1)
                top = jnp.where(lanes[k], moved, top)
            bottom = jnp.where(low_lane, pltpu.roll(top, bins - 2, 1), -pltpu.roll(top, 2, 1))
            out_ref[0, r, place, :] = top.astype(bf16)
            out_ref[0, r, below, :] = bottom.astype(bf16)


def circle(cycles):
    x = cycles - jnp.round(cycles)
    z = x * x * (math.pi * math.pi)
    sine, cosine = 0.0, 0.0
    for n in range(5, -1, -1):
        sine = sine * z + (-1.0) ** n / math.factorial(2 * n + 1)
    for n in range(6, -1, -1):
        cosine = cosine * z + (-1.0) ** n / math.factorial(2 * n)
    sine = sine * x * math.pi
    return 1.0 - 2.0 * sine * sine, 2.0 * sine * cosine


def turn(a, b):
    return a[0] * b[0] - a[1] * b[1], a[0] * b[1] + a[1] * b[0]


def spectra_kernel(blocks_here, samples, row_ref, blocks_ref, count_ref, green_ref, *refs):
    steps = (len(refs) - 2) // 2
    packed, outs, waves, total = refs[:steps], refs[steps : 2 * steps], refs[-2], refs[-1]
    variations, block_points = packed[0].shape[2:]
    bins = green_ref.shape[3]
    me = lax.axis_index("pt")
    lowest = me * blocks_here
    first_bin = (lax.axis_index("cmp") * bins).astype(f32)
    lane = lax.broadcasted_iota(jnp.int32, (variations, bins), 1)
    quarter = lane // 4
    for step in range(steps):
        source = packed[step]
        rupture = row_ref[jnp.bitwise_xor(me, step)]
        total[...] = jnp.zeros_like(total)

        def visit(slot, carry):
            local = blocks_ref[rupture, slot] - lowest

            @pl.when((local >= 0) & (local < blocks_here))
            def _():
                onset = source[local, 0].astype(f32) + source[local, 1].astype(f32)
                slip = source[local, 2].astype(f32)
                cycles = onset * (1.0 / samples)
                one = circle(cycles)
                two = turn(one, one)
                four = turn(two, two)
                start = circle(cycles * first_bin)
                now = [(slip * start[0], slip * start[1])]
                now.append(turn(now[0], one))
                now.append(turn(now[0], two))
                now.append(turn(now[1], two))
                after = [turn(wave, four) for wave in now]
                double = 2.0 * four[0]
                for j in range(bins // 4):
                    place = pl.ds(j * variations, variations)
                    for r in range(4):
                        waves[r, place, 0:block_points] = now[r][0].astype(bf16)
                        waves[r, place, block_points : 2 * block_points] = now[r][1].astype(bf16)
                    later = [
                        (double * after[r][0] - now[r][0], double * after[r][1] - now[r][1])
                        for r in range(4)
                    ]
                    now, after = after, later
                for r in range(4):
                    product = jnp.dot(waves[r], green_ref[local, r], preferred_element_type=f32)
                    found = product[0:variations]
                    for j in range(1, bins // 4):
                        found = jnp.where(
                            quarter == j, product[j * variations : (j + 1) * variations], found
                        )
                    total[r] += found

            return carry

        lax.fori_loop(0, count_ref[rupture], visit, 0)
        sums = [total[r] for r in range(4)]
        for k in range(4):
            spectrum = jnp.zeros_like(sums[0])
            for r in range(4):
                moved = sums[r] if k == r else pltpu.roll(sums[r], (r - k) % bins, 1)
                spectrum = jnp.where(lane % 4 == r, moved, spectrum)
            outs[step][k] = spectrum


def three_products(left, table_high, table_low):
    coarse = left.astype(bf16)
    fine = (left - coarse.astype(f32)).astype(bf16)
    return (
        jnp.dot(coarse, table_high, preferred_element_type=f32)
        + jnp.dot(fine, table_high, preferred_element_type=f32)
        + jnp.dot(coarse, table_low, preferred_element_type=f32)
    )


def half_sign(bins, columns):
    odd = lax.broadcasted_iota(jnp.int32, (1, columns), 1) % bins % 2
    return (1 - 2 * odd * lax.axis_index("cmp")).astype(f32)


def band_kernel(bins, high_ref, table_high, table_low, out_ref):
    rows = jnp.concatenate([high_ref[0, :, c, :] for c in range(2)], axis=0)
    band = three_products(rows, table_high[...], table_low[...])
    out_ref[...] = -band * half_sign(bins, 2 * bins)


def sum_kernel(bins_here, bins, band_ref, *refs):
    spectra, out_ref = refs[:-1], refs[-1]
    out_ref[...] = band_ref[...]
    half = lax.axis_index("cmp") * bins_here
    variations = spectra[0].shape[1]
    for k in range(4):
        piece = spectra[0][k]
        for other in spectra[1:]:
            piece = piece + other[k]
        place = pl.ds(pl.multiple_of((k // 2) * bins + half, bins_here), bins_here)
        rows = pl.ds((k % 2) * variations, variations)
        out_ref[rows, place] = out_ref[rows, place] + piece


def merge_kernel(
    bins, samples, row_ref, crossover_ref, own_ref, other_ref, high_ref, table_high, table_low, out_ref
):
    crossing = crossover_ref[row_ref[lax.axis_index("pt")]].astype(f32)
    column = lax.broadcasted_iota(jnp.int32, (1, 2 * bins), 1) % bins
    taper = jnp.clip((crossing - column.astype(f32)) / taper_width + 0.5, 0.0, 1.0)
    coefficient = jnp.where(column == 0, 1.0, 2.0) / samples
    weight = taper * coefficient * half_sign(bins, 2 * bins)
    excess = (own_ref[...] + other_ref[...]) * weight
    low = three_products(excess, table_high[...], table_low[...])
    variations = high_ref.shape[1]
    for c in range(2):
        out_ref[0, :, c, :] = high_ref[0, :, c, :] + low[c * variations : (c + 1) * variations]


def body(
    pt_size,
    strain_green,
    green_scale,
    mechanism,
    slip_amplitude,
    onset_time,
    rupture_row,
    rupture_blocks,
    block_count,
    crossover,
    high_band,
):
    points_here, strain_rows, bins_here = strain_green.shape
    blocks_here = green_scale.shape[0]
    block_points = points_here // blocks_here
    variations = slip_amplitude.shape[1]
    samples_here = high_band.shape[3]
    halves = 2
    bins = halves * bins_here
    samples = halves * samples_here
    assert slip_amplitude.shape[0] == 1 and pt_size & (pt_size - 1) == 0
    assert samples == 2 * bins and strain_rows == 24

    pack_shape = jax.ShapeDtypeStruct((blocks_here, 3, variations, block_points), bf16)
    packed = pl.pallas_call(
        functools.partial(pack_kernel, blocks_here, block_points),
        out_shape=[pack_shape] * pt_size,
        in_specs=[SMEM] * 3 + [VMEM] * 2,
        out_specs=[VMEM] * pt_size,
        compiler_params=params(),
        name="pack",
    )(rupture_row, rupture_blocks, block_count, slip_amplitude, onset_time)

    def swap(value, step):
        return lax.ppermute(value, "pt", [(i, i ^ step) for i in range(pt_size)])

    received = [packed[0]] + [swap(packed[step], step) for step in range(1, pt_size)]

    green = pl.pallas_call(
        green_kernel,
        grid=(blocks_here,),
        out_shape=jax.ShapeDtypeStruct((blocks_here, 4, 2 * block_points, bins_here), bf16),
        in_specs=[
            pl.BlockSpec((block_points * strain_rows, bins_here), lambda b: (b, 0)),
            pl.BlockSpec((1, 1, strain_rows), lambda b: (b, 0, 0)),
            pl.BlockSpec((6, block_points), lambda b: (0, b)),
        ],
        out_specs=pl.BlockSpec((1, 4, 2 * block_points, bins_here), lambda b: (b, 0, 0, 0)),
        compiler_params=params(),
        cost_estimate=cost(2 * points_here * strain_rows * bins_here, 6_000_000),
        name="green",
    )(
        strain_green.reshape(points_here * strain_rows, bins_here),
        green_scale.reshape(blocks_here, 1, strain_rows),
        mechanism,
    )

    spectrum_shape = jax.ShapeDtypeStruct((4, variations, bins_here), f32)
    spectra = pl.pallas_call(
        functools.partial(spectra_kernel, blocks_here, samples),
        out_shape=[spectrum_shape] * pt_size,
        in_specs=[SMEM] * 3 + [VMEM] * (1 + pt_size),
        out_specs=[VMEM] * pt_size,
        scratch_shapes=[
            pltpu.VMEM((4, variations * bins_here // 4, 2 * block_points), bf16),
            pltpu.VMEM((4, variations, bins_here), f32),
        ],
        compiler_params=params(),
        name="spectra",
    )(rupture_row, rupture_blocks, block_count, green, *received)

    gathered = [spectra[0]] + [swap(spectra[step], step) for step in range(1, pt_size)]

    table = fourier_table(bins, samples, samples_here)
    table_high, table_low = split_table(table)
    turned_high, turned_low = split_table(np.ascontiguousarray(table.T))
    rows = 2 * variations
    band = pl.pallas_call(
        functools.partial(band_kernel, bins),
        out_shape=jax.ShapeDtypeStruct((rows, 2 * bins), f32),
        in_specs=[VMEM] * 3,
        out_specs=VMEM,
        compiler_params=params(),
        cost_estimate=cost(6 * rows * samples_here * 2 * bins, 1_000_000),
        name="band",
    )(high_band, jnp.asarray(turned_high), jnp.asarray(turned_low))

    excess = pl.pallas_call(
        functools.partial(sum_kernel, bins_here, bins),
        out_shape=jax.ShapeDtypeStruct((rows, 2 * bins), f32),
        in_specs=[VMEM] * (1 + pt_size),
        out_specs=VMEM,
        compiler_params=params(),
        name="excess",
    )(band, *gathered)
    other = lax.ppermute(excess, "cmp", [(0, 1), (1, 0)])

    return pl.pallas_call(
        functools.partial(merge_kernel, bins, samples),
        out_shape=jax.ShapeDtypeStruct(high_band.shape, f32),
        in_specs=[SMEM] * 2 + [VMEM] * 5,
        out_specs=VMEM,
        compiler_params=params(),
        name="merge",
    )(rupture_row, crossover, excess, other, high_band, jnp.asarray(table_high), jnp.asarray(table_low))


def solution(mesh):
    assert mesh.shape["cmp"] == 2
    return jax.shard_map(
        functools.partial(body, mesh.shape["pt"]),
        mesh=mesh,
        in_specs=(
            P(("site", "pt"), None, "cmp"),
            P(("site", "pt"), None),
            P(None, "pt"),
            P("pt", "var", None),
            P("pt", "var", None),
            P(),
            P(),
            P(),
            P(),
            P(("site", "pt"), "var", None, "cmp"),
        ),
        out_specs=P(("site", "pt"), "var", None, "cmp"),
        check_vma=False,
    )
```

time: 168 us -> 34.8 us (0.21)
  other arithmetic: 33.2 us -> 0 us
  blocking collectives: 32.5 us -> 0 us
  local copies, waits for them, and re-layouts: 29.3 us -> 7.25 us
  matrix products: 19.6 us -> 0 us
  loops' own time: 18.1 us -> 0 us
  between operations: 16.2 us -> 0.12 us
  waiting for transfers between devices: 17.5 us -> 6.44 us
  starting transfers between devices: 0.04 us -> 10.5 us
  Pallas kernels: 0 us -> 10.1 us
    all_gather x3 -> x0, blocking collectives: 32.5 us -> none  [the longest x1 16.2 us: body(): lax.all_gather(onset_time, 'pt', axis=0, tiled=True)]
    reduce_sum x6 -> x0, other arithmetic: 28 us -> none  [the longest x5 27.3 us: block_term(): jnp.sum(with_cos * real_green + with_sin * imag_green, axis=1)]
    dot_general x4 -> x0, matrix products: 19.6 us -> none  [the longest x1 16.4 us: green_tensor(): jnp.einsum('pkjf,pkj->pkf', spectra, factors, precision=lax.Precision.HIG...]
    another operation x1 -> x0, loops' own time: 18.1 us -> none  [accumulate(): return lax.fori_loop(0, number_live, visit, running)]
    reduce_scatter x1 -> x0, waiting for transfers between devices: 11.5 us -> none  [body(): lax.psum_scatter(accumulate(initial, ordering, number_live, slot_total, f...]
    ppermute x0 -> x7, starting transfers between devices: none -> 10.5 us  [the longest x6 10.4 us: swap(): return lax.ppermute(value, 'pt', [(i, i ^ step) for i in range(pt_size)])]
    pallas_call x0 -> x6, Pallas kernels: none -> 10.1 us  [the longest x1 4.72 us: body(): pl.pallas_call(green_kernel, grid=(blocks_here,), out_shape=jax.ShapeDtyp...]
    unnamed x24 -> x32, local copies, waits for them, and re-layouts: 16.6 us -> 6.56 us
  transfers between devices with their start and end apart: 2 -> 7, of which waited for: 2 -> 3; matrix products, arithmetic and copies ran while one was open for 1% -> 2% of each run, Pallas kernels for 0% -> 14%
where the time goes in v1:
time: 34.8 us; the launch traced here: 34.4 us
  starting transfers between devices  10.5 us (30%)
  Pallas kernels  10.1 us (29%)
  local copies, waits for them, and re-layouts  7.25 us (21%)
  waiting for transfers between devices  6.44 us (19%)
    ppermute x6, starting transfers between devices, swap(): return lax.ppermute(value, 'pt', [(i, i ^ step) for i in range(pt_size)])  10.4 us
    unnamed x32, local copies, waits for them, and re-layouts  6.56 us
    ppermute x6, waiting for transfers between devices, swap(): return lax.ppermute(value, 'pt', [(i, i ^ step) for i in range(pt_size)])  5.2 us
    pallas_call x1, Pallas kernels, body(): pl.pallas_call(green_kernel, grid=(blocks_here,), out_shape=jax.ShapeDtyp...  4.72 us
    pallas_call x1, Pallas kernels, body(): pl.pallas_call(functools.partial(spectra_kernel, blocks_here, samples), o...  3.06 us
    pallas_call x1, Pallas kernels, body(): pl.pallas_call(functools.partial(merge_kernel, bins, samples), out_shape=...  1.41 us
    ppermute x1, waiting for transfers between devices, body(): other = lax.ppermute(excess, 'cmp', [(0, 1), (1, 0)])  1.24 us
  transfers between devices with their start and end apart: 7, of which 3 were waited for; matrix products, arithmetic and copies ran while one was open for 2% of the time, Pallas kernels for 14%

profile of v1, /device:TPU:0, one launch (start us, length us, event | category | flops | bytes accessed | tf_op | source)
XLA Modules:
  0.0 34.4 jit_solution(6989500296739608396)
XLA Ops:
  0.0 0.9 %copy-done.6 = f32[1,16,1536]{2,1,0:T(8,128)S(1)} copy-done((f32[1,16,1536]{2,1,0:T(8,128)S(1)}, f32[1,16,1536]{2,1,0:T(8,128)}, u32[]{:S(2)}) %copy-start.6) | copy-done | bytes 98328
  0.9 0.8 %copy-done.7 = bf16[1,16,1536]{2,1,0:T(8,128)(2,1)S(1)} copy-done((bf16[1,16,1536]{2,1,0:T(8,128)(2,1)S(1)}, bf16[1,16,1536]{2,1,0:T(8,128)(2,1)}, u32[]{:S(2)}) %copy-start.7) | copy-done | bytes 49176
  1.7 0.7 %copy-done.9 = s32[4,12]{1,0:T(4,128)S(1)} copy-done((s32[4,12]{1,0:T(4,128)S(1)}, s32[4,12]{1,0:T(4,128)}, u32[]{:S(2)}) %copy-start.9) | copy-done | bytes 216
  2.4 0.7 %copy-done.11 = s32[4]{0:T(128)S(1)} copy-done((s32[4]{0:T(128)S(1)}, s32[4]{0:T(128)}, u32[]{:S(2)}) %copy-start.11) | copy-done | bytes 40
  3.0 0.7 %copy-done.13 = s32[4]{0:T(128)S(1)} copy-done((s32[4]{0:T(128)S(1)}, s32[4]{0:T(128)}, u32[]{:S(2)}) %copy-start.13) | copy-done | bytes 40
  3.7 0.6 %pack.1 = (bf16[5,3,16,128]{3,2,1,0:T(8,128)(2,1)S(1)}, bf16[5,3,16,128]{3,2,1,0:T(8,128)(2,1)S(1)}, bf16[5,3,16,128]{3,2,1,0:T(8,128)(2,1)S(1)}, bf16[5,3,16,128]{3,2,1,0:T(8,128)(2,1)S(1)}) custom-call(s32[4]{0:T(128)S(1)} %copy-done.11, s32[4,12]{1,0:T(4,128)S(1)} %copy-done.9, s32[4]{0:T(128)S(1)} %copy-done.13, bf16[1,16,1536]{2,1,0:T(8,128)(2,1)S(1)} %copy-done.7, ...), custom_call_target="tpu_custom_call" | custom-call | tf_op jit(solution)/shard_map/pack/pallas_call | solution.py:277
  4.4 3.6 %collective-permute-start = (bf16[5,3,16,128]{3,2,1,0:T(8,128)(2,1)S(1)}, bf16[5,3,16,128]{3,2,1,0:T(8,128)(2,1)S(1)}, u32[]{:S(2)}, u32[]{:S(2)}) collective-permute-start(bf16[5,3,16,128]{3,2,1,0:T(8,128)(2,1)S(1)} %get-tuple-element.14), channel_id=1, source_target_pairs={{0,4},{4,0},{8,12},{12,8},{1,5},{5,1},{9,13},{13,9},{2,6},{6,2},{1... | collective-permute-start | bytes 184328 | tf_op jit(solution)/shard_map/ppermute | solution.py:287
  7.9 2.2 %collective-permute-start.1 = (bf16[5,3,16,128]{3,2,1,0:T(8,128)(2,1)S(1)}, bf16[5,3,16,128]{3,2,1,0:T(8,128)(2,1)S(1)}, u32[]{:S(2)}, u32[]{:S(2)}) collective-permute-start(bf16[5,3,16,128]{3,2,1,0:T(8,128)(2,1)S(1)} %get-tuple-element.15), channel_id=1, source_target_pairs={{0,8},{4,12},{8,0},{12,4},{1,9},{5,13},{9,1},{13,5},{2,10},{6,14},... | collective-permute-start | bytes 184328 | tf_op jit(solution)/shard_map/ppermute | solution.py:287
  10.1 0.3 collective-permute-start.2
  10.3 0.7 %copy.15.scale_ref = f32[5,1,24]{2,1,0:T(1,128)S(1)} copy(f32[5,1,24]{2,0,1:T(8,128)} %bitcast.3) | data formatting | bytes 960 | tf_op jit(solution)/shard_map/reshape | solution.py:306
  11.0 2.1 %copy-done = bf16[640,24,128]{2,1,0:T(8,128)(2,1)S(1)} copy-done((bf16[640,24,128]{2,1,0:T(8,128)(2,1)S(1)}, bf16[640,24,128]{2,1,0:T(8,128)(2,1)}, u32[]{:S(2)}) %copy-start) | copy-done | bytes 3932184
  13.2 0.7 %copy-done.8 = f32[6,640]{1,0:T(8,128)S(1)} copy-done((f32[6,640]{1,0:T(8,128)S(1)}, f32[6,640]{1,0:T(8,128)}, u32[]{:S(2)}) %copy-start.8) | copy-done | bytes 15384
  13.9 4.7 %green.1.green_ref = bf16[5,4,256,128]{3,2,1,0:T(8,128)(2,1)S(1)} custom-call(bf16[15360,128]{1,0:T(8,128)(2,1)S(1)} %bitcast.2, f32[5,1,24]{2,1,0:T(1,128)S(1)} %copy.15.scale_ref, f32[6,640]{1,0:T(8,128)S(1)} %copy-done.8), custom_call_target="tpu_custom_call" | custom-call | flops 3932160 | bytes 6000000 | tf_op jit(solution)/shard_map/green/pallas_call | solution.py:291
  18.7 3.1 %spectra.1 = (f32[4,16,128]{2,1,0:T(8,128)S(1)}, f32[4,16,128]{2,1,0:T(8,128)S(1)}, f32[4,16,128]{2,1,0:T(8,128)S(1)}, f32[4,16,128]{2,1,0:T(8,128)S(1)}) custom-call(s32[4]{0:T(128)S(1)} %copy-done.12, s32[4,12]{1,0:T(4,128)S(1)} %copy-done.10, s32[4]{0:T(128)S(1)} %copy-done.14, bf16[5,4,256,128]{3,2,1,0:T(8,128)(2,1)S(1)} %green.1.green_ref, ...), custom_call_target="tpu_custom_call" | custom-call | tf_op jit(solution)/shard_map/spectra/pallas_call | solution.py:311
  21.7 1.1 %collective-permute-start.3 = (f32[4,16,128]{2,1,0:T(8,128)S(1)}, f32[4,16,128]{2,1,0:T(8,128)S(1)}, u32[]{:S(2)}, u32[]{:S(2)}) collective-permute-start(f32[4,16,128]{2,1,0:T(8,128)S(1)} %get-tuple-element.18), channel_id=1, source_target_pairs={{0,4},{4,0},{8,12},{12,8},{1,5},{5,1},{9,13},{13,9},{2,6},{6,2},{1... | collective-permute-start | bytes 98312 | tf_op jit(solution)/shard_map/ppermute | solution.py:287
  22.8 3.1 %collective-permute-start.4 = (f32[4,16,128]{2,1,0:T(8,128)S(1)}, f32[4,16,128]{2,1,0:T(8,128)S(1)}, u32[]{:S(2)}, u32[]{:S(2)}) collective-permute-start(f32[4,16,128]{2,1,0:T(8,128)S(1)} %get-tuple-element.19), channel_id=1, source_target_pairs={{0,8},{4,12},{8,0},{12,4},{1,9},{5,13},{9,1},{13,5},{2,10},{6,14},... | collective-permute-start | bytes 98312 | tf_op jit(solution)/shard_map/ppermute | solution.py:287
  25.9 0.3 collective-permute-start.5
  26.2 0.2 band.1.band_ref
  26.4 0.0 collective-permute-done.3.refs_1_
  26.5 1.4 %collective-permute-done.4.refs_2_ = f32[4,16,128]{2,1,0:T(8,128)S(1)} collective-permute-done((f32[4,16,128]{2,1,0:T(8,128)S(1)}, f32[4,16,128]{2,1,0:T(8,128)S(1)}, u32[]{:S(2)}, u32[]{:S(2)}) %collective-permute-start.4) | collective-permute-done | bytes 32800 | tf_op jit(solution)/shard_map/ppermute | solution.py:287
  27.8 3.8 %collective-permute-done.5.refs_3_ = f32[4,16,128]{2,1,0:T(8,128)S(1)} collective-permute-done((f32[4,16,128]{2,1,0:T(8,128)S(1)}, f32[4,16,128]{2,1,0:T(8,128)S(1)}, u32[]{:S(2)}, u32[]{:S(2)}) %collective-permute-start.5) | collective-permute-done | bytes 32800 | tf_op jit(solution)/shard_map/ppermute | solution.py:287
  31.7 0.1 collective-permute-start.6
  31.7 1.2 %collective-permute-done.6.other_ref = f32[32,512]{1,0:T(8,128)S(1)} collective-permute-done((f32[32,512]{1,0:T(8,128)S(1)}, f32[32,512]{1,0:T(8,128)S(1)}, u32[]{:S(2)}, u32[]{:S(2)}) %collective-permute-start.6) | collective-permute-done | bytes 65568 | tf_op jit(solution)/shard_map/ppermute | solution.py:348
  33.0 1.4 %merge.1 = f32[1,16,2,256]{3,2,1,0:T(2,128)} custom-call(s32[4]{0:T(128)S(1)} %copy-done.12, s32[4]{0:T(128)S(1)} %copy-done.15, f32[32,512]{1,0:T(8,128)S(1)} %excess.1.own_ref, f32[32,512]{1,0:T(8,128)S(1)} %collective-permute-done.6.other_ref, f32[1,16,2,256]{3,2,1,0:T(2,128)S(1)} %copy-done.5, bf16[512,256]{1,0:T(8,128)(2,1)S(1)} %copy-done.1, ...), custom_call_target="tpu_custom_call" | custom-call | tf_op jit(solution)/shard_map/merge/pallas_call | solution.py:350
  (29 shorter events, 0.1 us)
Async XLA Ops:
  0.0 26.2 %copy-start.5 = (f32[1,16,2,256]{3,2,1,0:T(2,128)S(1)}, f32[1,16,2,256]{3,2,1,0:T(2,128)}, u32[]{:S(2)}) copy-start(f32[1,16,2,256]{3,2,1,0:T(2,128)} %high_ref.3) | copy-start | bytes 98308
  0.0 0.9 %copy-start.6 = (f32[1,16,1536]{2,1,0:T(8,128)S(1)}, f32[1,16,1536]{2,1,0:T(8,128)}, u32[]{:S(2)}) copy-start(f32[1,16,1536]{2,1,0:T(8,128)} %onset_ref.1) | copy-start | bytes 294916
  0.9 0.8 %copy-start.7 = (bf16[1,16,1536]{2,1,0:T(8,128)(2,1)S(1)}, bf16[1,16,1536]{2,1,0:T(8,128)(2,1)}, u32[]{:S(2)}) copy-start(bf16[1,16,1536]{2,1,0:T(8,128)(2,1)} %slip_ref.1) | copy-start | bytes 147460
  1.7 0.7 %copy-start.9 = (s32[4,12]{1,0:T(4,128)S(1)}, s32[4,12]{1,0:T(4,128)}, u32[]{:S(2)}) copy-start(s32[4,12]{1,0:T(4,128)} %blocks_ref.3) | copy-start | bytes 580
  2.4 0.7 %copy-start.11 = (s32[4]{0:T(128)S(1)}, s32[4]{0:T(128)}, u32[]{:S(2)}) copy-start(s32[4]{0:T(128)} %row_ref.5) | copy-start | bytes 52
  3.0 0.7 %copy-start.13 = (s32[4]{0:T(128)S(1)}, s32[4]{0:T(128)}, u32[]{:S(2)}) copy-start(s32[4]{0:T(128)} %count_ref.3) | copy-start | bytes 52
  3.7 15.0 %copy-start.10 = (s32[4,12]{1,0:T(4,128)S(1)}, s32[4,12]{1,0:T(4,128)}, u32[]{:S(2)}) copy-start(s32[4,12]{1,0:T(4,128)} %blocks_ref.3) | copy-start | bytes 580
  3.7 15.0 %copy-start.12 = (s32[4]{0:T(128)S(1)}, s32[4]{0:T(128)}, u32[]{:S(2)}) copy-start(s32[4]{0:T(128)} %row_ref.5) | copy-start | bytes 52
  3.7 15.0 %copy-start.14 = (s32[4]{0:T(128)S(1)}, s32[4]{0:T(128)}, u32[]{:S(2)}) copy-start(s32[4]{0:T(128)} %count_ref.3) | copy-start | bytes 52
  3.7 29.3 %copy-start.15 = (s32[4]{0:T(128)S(1)}, s32[4]{0:T(128)}, u32[]{:S(2)}) copy-start(s32[4]{0:T(128)} %crossover_ref.1) | copy-start | bytes 52
  4.4 14.3 %collective-permute-start = (bf16[5,3,16,128]{3,2,1,0:T(8,128)(2,1)S(1)}, bf16[5,3,16,128]{3,2,1,0:T(8,128)(2,1)S(1)}, u32[]{:S(2)}, u32[]{:S(2)}) collective-permute-start(bf16[5,3,16,128]{3,2,1,0:T(8,128)(2,1)S(1)} %get-tuple-element.14), channel_id=1, source_target_pairs={{0,4},{4,0},{8,12},{12,8},{1,5},{5,1},{9,13},{13,9},{2,6},{6,2},{1... | collective-permute-start | bytes 184328 | tf_op jit(solution)/shard_map/ppermute | solution.py:287
  7.9 10.7 %collective-permute-start.1 = (bf16[5,3,16,128]{3,2,1,0:T(8,128)(2,1)S(1)}, bf16[5,3,16,128]{3,2,1,0:T(8,128)(2,1)S(1)}, u32[]{:S(2)}, u32[]{:S(2)}) collective-permute-start(bf16[5,3,16,128]{3,2,1,0:T(8,128)(2,1)S(1)} %get-tuple-element.15), channel_id=1, source_target_pairs={{0,8},{4,12},{8,0},{12,4},{1,9},{5,13},{9,1},{13,5},{2,10},{6,14},... | collective-permute-start | bytes 184328 | tf_op jit(solution)/shard_map/ppermute | solution.py:287
  10.1 8.6 %collective-permute-start.2 = (bf16[5,3,16,128]{3,2,1,0:T(8,128)(2,1)S(1)}, bf16[5,3,16,128]{3,2,1,0:T(8,128)(2,1)S(1)}, u32[]{:S(2)}, u32[]{:S(2)}) collective-permute-start(bf16[5,3,16,128]{3,2,1,0:T(8,128)(2,1)S(1)} %get-tuple-element.16), channel_id=1, source_target_pairs={{0,12},{4,8},{8,4},{12,0},{1,13},{5,9},{9,5},{13,1},{2,14},{6,10},... | collective-permute-start | bytes 184328 | tf_op jit(solution)/shard_map/ppermute | solution.py:287
  11.0 2.1 %copy-start = (bf16[640,24,128]{2,1,0:T(8,128)(2,1)S(1)}, bf16[640,24,128]{2,1,0:T(8,128)(2,1)}, u32[]{:S(2)}) copy-start(bf16[640,24,128]{2,1,0:T(8,128)(2,1)} %param.14) | copy-start | bytes 11796484
  13.1 0.7 %copy-start.8 = (f32[6,640]{1,0:T(8,128)S(1)}, f32[6,640]{1,0:T(8,128)}, u32[]{:S(2)}) copy-start(f32[6,640]{1,0:T(8,128)} %mechanism_ref.1) | copy-start | bytes 46084
  13.9 12.3 %copy-start.3 = (bf16[256,512]{1,0:T(8,128)(2,1)S(1)}, bf16[256,512]{1,0:T(8,128)(2,1)}, u32[]{:S(2)}) copy-start(bf16[256,512]{1,0:T(8,128)(2,1)} %constant.8.clone.table_high) | copy-start | bytes 786436
  13.9 12.3 %copy-start.4 = (bf16[256,512]{1,0:T(8,128)(2,1)S(1)}, bf16[256,512]{1,0:T(8,128)(2,1)}, u32[]{:S(2)}) copy-start(bf16[256,512]{1,0:T(8,128)(2,1)} %constant.9.clone.table_low) | copy-start | bytes 786436
  13.9 19.1 %copy-start.1 = (bf16[512,256]{1,0:T(8,128)(2,1)S(1)}, bf16[512,256]{1,0:T(8,128)(2,1)}, u32[]{:S(2)}) copy-start(bf16[512,256]{1,0:T(8,128)(2,1)} %constant.10.clone.table_high) | copy-start | bytes 786436
  13.9 19.1 %copy-start.2 = (bf16[512,256]{1,0:T(8,128)(2,1)S(1)}, bf16[512,256]{1,0:T(8,128)(2,1)}, u32[]{:S(2)}) copy-start(bf16[512,256]{1,0:T(8,128)(2,1)} %constant.11.clone.table_low) | copy-start | bytes 786436
  21.7 4.7 %collective-permute-start.3 = (f32[4,16,128]{2,1,0:T(8,128)S(1)}, f32[4,16,128]{2,1,0:T(8,128)S(1)}, u32[]{:S(2)}, u32[]{:S(2)}) collective-permute-start(f32[4,16,128]{2,1,0:T(8,128)S(1)} %get-tuple-element.18), channel_id=1, source_target_pairs={{0,4},{4,0},{8,12},{12,8},{1,5},{5,1},{9,13},{13,9},{2,6},{6,2},{1... | collective-permute-start | bytes 98312 | tf_op jit(solution)/shard_map/ppermute | solution.py:287
  22.8 5.0 %collective-permute-start.4 = (f32[4,16,128]{2,1,0:T(8,128)S(1)}, f32[4,16,128]{2,1,0:T(8,128)S(1)}, u32[]{:S(2)}, u32[]{:S(2)}) collective-permute-start(f32[4,16,128]{2,1,0:T(8,128)S(1)} %get-tuple-element.19), channel_id=1, source_target_pairs={{0,8},{4,12},{8,0},{12,4},{1,9},{5,13},{9,1},{13,5},{2,10},{6,14},... | collective-permute-start | bytes 98312 | tf_op jit(solution)/shard_map/ppermute | solution.py:287
  25.9 5.7 %collective-permute-start.5 = (f32[4,16,128]{2,1,0:T(8,128)S(1)}, f32[4,16,128]{2,1,0:T(8,128)S(1)}, u32[]{:S(2)}, u32[]{:S(2)}) collective-permute-start(f32[4,16,128]{2,1,0:T(8,128)S(1)} %get-tuple-element.20), channel_id=1, source_target_pairs={{0,12},{4,8},{8,4},{12,0},{1,13},{5,9},{9,5},{13,1},{2,14},{6,10},... | collective-permute-start | bytes 98312 | tf_op jit(solution)/shard_map/ppermute | solution.py:287
  31.7 1.3 %collective-permute-start.6 = (f32[32,512]{1,0:T(8,128)S(1)}, f32[32,512]{1,0:T(8,128)S(1)}, u32[]{:S(2)}, u32[]{:S(2)}) collective-permute-start(f32[32,512]{1,0:T(8,128)S(1)} %excess.1.own_ref), channel_id=1, source_target_pairs={{0,1},{1,0},{2,3},{3,2},{4,5},{5,4},{6,7},{7,6},{8,9},{9,8},{10,11... | collective-permute-start | bytes 196616 | tf_op jit(solution)/shard_map/ppermute | solution.py:348

commit v2 on v1

--- a/solution.py
+++ b/solution.py
@@ -14,9 +14,24 @@
 f32 = jnp.float32
 bf16 = jnp.bfloat16
 highest = lax.Precision.HIGHEST
-vmem_bytes = 48 * 1024 * 1024
+vmem_bytes = 32 * 1024 * 1024
 SMEM = pl.BlockSpec(memory_space=pltpu.SMEM)
 VMEM = pl.BlockSpec(memory_space=pltpu.VMEM)
+HBM = pl.BlockSpec(memory_space=pltpu.HBM)
+
+
+def in_hbm(*arrays):
+    return [pltpu.with_memory_space_constraint(array, pltpu.HBM) for array in arrays]
+
+
+def fetch(sources, targets, sems):
+    copies = [
+        pltpu.make_async_copy(source, target, sems.at[i])
+        for i, (source, target) in enumerate(zip(sources, targets))
+    ]
+    for copy in copies:
+        copy.start()
+    return copies
 
 
 def params():
@@ -39,7 +54,15 @@
     return np.concatenate([np.cos(angle), -np.sin(angle)], axis=0)
 
 
-def pack_kernel(blocks_here, block_points, row_ref, blocks_ref, count_ref, slip_ref, onset_ref, *outs):
+def pack_kernel(blocks_here, block_points, *refs):
+    sources, strain_hbm, outs, head_ref = refs[:5], refs[5], refs[6:-8], refs[-8]
+    targets, sems, head_sem = refs[-7:-2], refs[-2], refs[-1]
+    row_ref, blocks_ref, count_ref, slip_ref, onset_ref = targets
+    copies = fetch(sources, targets, sems)
+    head = pltpu.make_async_copy(strain_hbm.at[pl.ds(0, head_ref.shape[0])], head_ref, head_sem)
+    head.start()
+    for copy in copies:
+        copy.wait()
     me = lax.axis_index("pt")
     rupture = row_ref[me]
 
@@ -63,60 +86,103 @@
         return carry
 
     lax.fori_loop(0, count_ref[rupture], visit, 0)
-
-
-def green_kernel(strain_ref, scale_ref, mechanism_ref, out_ref):
-    block_points, bins = mechanism_ref.shape[1], strain_ref.shape[1]
-    rows = 24
-    octet = 8
+    head.wait()
+
+
+def three_parts(values):
+    parts = []
+    for _ in range(3):
+        parts.append(values.astype(bf16).astype(f32))
+        values = values - parts[-1]
+    return parts
+
+
+def green_kernel(
+    head_ref, strain_hbm, scale_hbm, mechanism_hbm, out_ref, strain_ref, factor_ref, scale_ref, mechanism_ref, sems, small_sems
+):
+    small = fetch((scale_hbm, mechanism_hbm), (scale_ref, mechanism_ref), small_sems)
+    rows, octet = 24, 8
     wide = octet * rows
-    column = lax.broadcasted_iota(jnp.int32, (6, wide), 1) % rows
-    spread_six = (column % 6 == lax.broadcasted_iota(jnp.int32, (6, wide), 0)).astype(f32)
-    column = lax.broadcasted_iota(jnp.int32, (rows, wide), 1) % rows
-    spread_rows = (column == lax.broadcasted_iota(jnp.int32, (rows, wide), 0)).astype(f32)
+    blocks_here = scale_ref.shape[0]
+    bins = strain_ref.shape[1]
+    block_points = mechanism_ref.shape[1] // blocks_here
+    per_block = block_points * rows
+
+    def strain_copy(b, source=strain_hbm):
+        place = pl.ds(pl.multiple_of(b * per_block, per_block), per_block)
+        return pltpu.make_async_copy(source.at[place], strain_ref.at[place], sems.at[b])
+
+    for b in range(blocks_here):
+        strain_copy(b, head_ref if b * per_block < head_ref.shape[0] else strain_hbm).start()
+    for copy in small:
+        copy.wait()
+    column = lax.broadcasted_iota(jnp.int32, (18, wide), 1) % rows
+    spread_six = column % 6 == lax.broadcasted_iota(jnp.int32, (18, wide), 0) % 6
+    column = lax.broadcasted_iota(jnp.int32, (3 * rows, wide), 1) % rows
+    spread_rows = column == lax.broadcasted_iota(jnp.int32, (3 * rows, wide), 0) % rows
     moments = lax.dot_general(
-        mechanism_ref[...], spread_six, (((0,), (0,)), ((), ())), precision=highest,
+        jnp.concatenate(three_parts(mechanism_ref[...]), axis=0).astype(bf16),
+        spread_six.astype(f32).astype(bf16),
+        (((0,), (0,)), ((), ())),
         preferred_element_type=f32,
     )
-    scales = jnp.dot(scale_ref[0], spread_rows, precision=highest, preferred_element_type=f32)
-    factor = moments * scales
-    column = lax.broadcasted_iota(jnp.int32, (octet, wide), 1)
-    same_point = column // rows == lax.broadcasted_iota(jnp.int32, (octet, wide), 0)
+    scales = jnp.dot(
+        jnp.concatenate(three_parts(scale_ref[...]), axis=1).astype(bf16),
+        spread_rows.astype(f32).astype(bf16),
+        preferred_element_type=f32,
+    )
+    for b in range(blocks_here):
+        place = slice(b * block_points, (b + 1) * block_points)
+        factor_ref[place, :] = moments[place] * scales[b : b + 1]
+    row = lax.broadcasted_iota(jnp.int32, (2 * octet, wide), 0)
+    column = lax.broadcasted_iota(jnp.int32, (2 * octet, wide), 1)
+    same_point = column // rows == row % octet
     part = (column % rows) // 6
-    masks = [same_point & (part == k) for k in range(4)]
+    masks = [
+        jnp.where(same_point & (part == 2 * h + row // octet), 1.0, 0.0).astype(bf16)
+        for h in range(2)
+    ]
     lane = lax.broadcasted_iota(jnp.int32, (2 * octet, bins), 1) % 4
     lanes = [lane == k for k in range(4)]
     low_lane = lane < 2
-    for pair in range(block_points // (2 * octet)):
-        spectra = [[], [], [], []]
-        for half in range(2):
-            first = pair * 2 * octet + half * octet
-            here = factor[first : first + octet]
-            coarse = here.astype(bf16).astype(f32)
-            fine = here - coarse
-            left = jnp.concatenate(
-                [jnp.where(mask, coarse, 0.0) for mask in masks]
-                + [jnp.where(mask, fine, 0.0) for mask in masks],
-                axis=0,
-            ).astype(bf16)
-            strain = strain_ref[first * rows : first * rows + wide, :]
-            both = jnp.dot(left, strain, preferred_element_type=f32)
-            for k in range(4):
-                spectra[k].append(
-                    both[k * octet : (k + 1) * octet]
-                    + both[(k + 4) * octet : (k + 5) * octet]
+
+    def one_block(b, carry):
+        strain_copy(b).wait()
+        for pair in range(block_points // (2 * octet)):
+            spectra = [[], [], [], []]
+            for half in range(2):
+                first = pl.multiple_of(
+                    b * block_points + pair * 2 * octet + half * octet, octet
                 )
-        green = [jnp.concatenate(s, axis=0).astype(bf16).astype(f32) for s in spectra]
-        place = pl.ds(pair * 2 * octet, 2 * octet)
-        below = pl.ds(block_points + pair * 2 * octet, 2 * octet)
-        for r in range(4):
-            top = jnp.zeros_like(green[0])
-            for k in range(4):
-                moved = green[k] if k == r else pltpu.roll(green[k], (k - r) % bins, 1)
-                top = jnp.where(lanes[k], moved, top)
-            bottom = jnp.where(low_lane, pltpu.roll(top, bins - 2, 1), -pltpu.roll(top, 2, 1))
-            out_ref[0, r, place, :] = top.astype(bf16)
-            out_ref[0, r, below, :] = bottom.astype(bf16)
+                here = factor_ref[pl.ds(first, octet)]
+                here = jnp.concatenate([here, here], axis=0)
+                coarse = here.astype(bf16)
+                fine = (here - coarse.astype(f32)).astype(bf16)
+                left = jnp.concatenate(
+                    [coarse * masks[0], coarse * masks[1], fine * masks[0], fine * masks[1]],
+                    axis=0,
+                )
+                strain = strain_ref[pl.ds(pl.multiple_of(first * rows, wide), wide), :]
+                both = jnp.dot(left, strain, preferred_element_type=f32)
+                for k in range(4):
+                    spectra[k].append(
+                        both[k * octet : (k + 1) * octet]
+                        + both[(k + 4) * octet : (k + 5) * octet]
+                    )
+            green = [jnp.concatenate(s, axis=0).astype(bf16).astype(f32) for s in spectra]
+            place = pl.ds(pair * 2 * octet, 2 * octet)
+            below = pl.ds(block_points + pair * 2 * octet, 2 * octet)
+            for r in range(4):
+                top = green[0] if r == 0 else pltpu.roll(green[0], bins - r, 1)
+                for k in range(1, 4):
+                    moved = green[k] if k == r else pltpu.roll(green[k], (k - r) % bins, 1)
+                    top = jnp.where(lanes[k], moved, top)
+                bottom = jnp.where(low_lane, pltpu.roll(top, bins - 2, 1), -pltpu.roll(top, 2, 1))
+                out_ref[b, r, place, :] = top.astype(bf16)
+                out_ref[b, r, below, :] = bottom.astype(bf16)
+        return carry
+
+    lax.fori_loop(0, blocks_here, one_block, 0)
 
 
 def circle(cycles):
@@ -135,9 +201,11 @@
     return a[0] * b[0] - a[1] * b[1], a[0] * b[1] + a[1] * b[0]
 
 
-def spectra_kernel(blocks_here, samples, row_ref, blocks_ref, count_ref, green_ref, *refs):
-    steps = (len(refs) - 2) // 2
-    packed, outs, waves, total = refs[:steps], refs[steps : 2 * steps], refs[-2], refs[-1]
+def spectra_kernel(blocks_here, samples, row_hbm, blocks_hbm, count_hbm, green_ref, *refs):
+    steps = (len(refs) - 7) // 2
+    packed, outs = refs[:steps][::-1], refs[steps : 2 * steps]
+    waves, total, held, row_ref, blocks_ref, count_ref, sems = refs[-7:]
+    scalars = fetch((row_hbm, blocks_hbm, count_hbm), (row_ref, blocks_ref, count_ref), sems)
     variations, block_points = packed[0].shape[2:]
     bins = green_ref.shape[3]
     me = lax.axis_index("pt")
@@ -145,18 +213,22 @@
     first_bin = (lax.axis_index("cmp") * bins).astype(f32)
     lane = lax.broadcasted_iota(jnp.int32, (variations, bins), 1)
     quarter = lane // 4
+    total[...] = jnp.zeros_like(total)
     for step in range(steps):
-        source = packed[step]
+        held[step] = packed[step][...]
+    for copy in scalars:
+        copy.wait()
+
+    def one_row(step, carry):
         rupture = row_ref[jnp.bitwise_xor(me, step)]
-        total[...] = jnp.zeros_like(total)
 
         def visit(slot, carry):
             local = blocks_ref[rupture, slot] - lowest
 
             @pl.when((local >= 0) & (local < blocks_here))
             def _():
-                onset = source[local, 0].astype(f32) + source[local, 1].astype(f32)
-                slip = source[local, 2].astype(f32)
+                onset = held[step, local, 0].astype(f32) + held[step, local, 1].astype(f32)
+                slip = held[step, local, 2].astype(f32)
                 cycles = onset * (1.0 / samples)
                 one = circle(cycles)
                 two = turn(one, one)
@@ -185,18 +257,48 @@
                         found = jnp.where(
                             quarter == j, product[j * variations : (j + 1) * variations], found
                         )
-                    total[r] += found
+                    total[step, r] += found
 
             return carry
 
-        lax.fori_loop(0, count_ref[rupture], visit, 0)
-        sums = [total[r] for r in range(4)]
+        return lax.fori_loop(0, count_ref[rupture], visit, carry)
+
+    lax.fori_loop(0, steps, one_row, 0)
+    for step in range(steps):
+        sums = [total[step, r] for r in range(4)]
         for k in range(4):
-            spectrum = jnp.zeros_like(sums[0])
-            for r in range(4):
+            spectrum = sums[0] if k == 0 else pltpu.roll(sums[0], bins - k, 1)
+            for r in range(1, 4):
                 moved = sums[r] if k == r else pltpu.roll(sums[r], (r - k) % bins, 1)
                 spectrum = jnp.where(lane % 4 == r, moved, spectrum)
             outs[step][k] = spectrum
+
+
+def scalar_scratch(arrays):
+    return [pltpu.SMEM(array.shape, array.dtype) for array in arrays]
+
+
+def spectra_call(rupture_row, rupture_blocks, block_count, green, received):
+    pt_size = len(received)
+    blocks_here, parts, variations, block_points = received[0].shape
+    bins_here = green.shape[3]
+    samples = 4 * bins_here
+    scalars = (rupture_row, rupture_blocks, block_count)
+    return pl.pallas_call(
+        functools.partial(spectra_kernel, blocks_here, samples),
+        out_shape=[jax.ShapeDtypeStruct((4, variations, bins_here), f32)] * pt_size,
+        in_specs=[HBM] * 3 + [VMEM] * (1 + pt_size),
+        out_specs=[VMEM] * pt_size,
+        scratch_shapes=[
+            pltpu.VMEM((4, variations * bins_here // 4, 2 * block_points), bf16),
+            pltpu.VMEM((pt_size, 4, variations, bins_here), f32),
+            pltpu.VMEM((pt_size, blocks_here, parts, variations, block_points), bf16),
+        ]
+        + scalar_scratch(scalars)
+        + [pltpu.SemaphoreType.DMA((3,))],
+        compiler_params=params(),
+        name="spectra",
+    )(*in_hbm(*scalars), green, *received[::-1])
 
 
 def three_products(left, table_high, table_low):
@@ -273,55 +375,55 @@
     assert slip_amplitude.shape[0] == 1 and pt_size & (pt_size - 1) == 0
     assert samples == 2 * bins and strain_rows == 24
 
+    strain_lines = strain_green.reshape(points_here * strain_rows, bins_here)
+    head_blocks = 1
+    head_shape = jax.ShapeDtypeStruct((head_blocks * block_points * strain_rows, bins_here), bf16)
     pack_shape = jax.ShapeDtypeStruct((blocks_here, 3, variations, block_points), bf16)
-    packed = pl.pallas_call(
+    *packed, head = pl.pallas_call(
         functools.partial(pack_kernel, blocks_here, block_points),
-        out_shape=[pack_shape] * pt_size,
-        in_specs=[SMEM] * 3 + [VMEM] * 2,
-        out_specs=[VMEM] * pt_size,
+        out_shape=[pack_shape] * pt_size + [head_shape],
+        in_specs=[HBM] * 6,
+        out_specs=[VMEM] * (pt_size + 1),
+        scratch_shapes=scalar_scratch((rupture_row, rupture_blocks, block_count))
+        + [pltpu.VMEM(a.shape, a.dtype) for a in (slip_amplitude, onset_time)]
+        + [pltpu.SemaphoreType.DMA((5,)), pltpu.SemaphoreType.DMA],
         compiler_params=params(),
         name="pack",
-    )(rupture_row, rupture_blocks, block_count, slip_amplitude, onset_time)
+    )(
+        *in_hbm(
+            rupture_row, rupture_blocks, block_count, slip_amplitude, onset_time, strain_lines
+        )
+    )
 
     def swap(value, step):
         return lax.ppermute(value, "pt", [(i, i ^ step) for i in range(pt_size)])
 
-    received = [packed[0]] + [swap(packed[step], step) for step in range(1, pt_size)]
+    def exchange(values):
+        moved = [swap(values[step], step) for step in range(pt_size - 1, 0, -1)]
+        return [values[0]] + moved[::-1]
+
+    received = exchange(packed)
 
     green = pl.pallas_call(
         green_kernel,
-        grid=(blocks_here,),
         out_shape=jax.ShapeDtypeStruct((blocks_here, 4, 2 * block_points, bins_here), bf16),
-        in_specs=[
-            pl.BlockSpec((block_points * strain_rows, bins_here), lambda b: (b, 0)),
-            pl.BlockSpec((1, 1, strain_rows), lambda b: (b, 0, 0)),
-            pl.BlockSpec((6, block_points), lambda b: (0, b)),
+        in_specs=[VMEM] + [HBM] * 3,
+        out_specs=VMEM,
+        scratch_shapes=[
+            pltpu.VMEM(strain_lines.shape, bf16),
+            pltpu.VMEM((points_here, 8 * strain_rows), f32),
+            pltpu.VMEM(green_scale.shape, f32),
+            pltpu.VMEM(mechanism.shape, f32),
+            pltpu.SemaphoreType.DMA((blocks_here,)),
+            pltpu.SemaphoreType.DMA((2,)),
         ],
-        out_specs=pl.BlockSpec((1, 4, 2 * block_points, bins_here), lambda b: (b, 0, 0, 0)),
         compiler_params=params(),
         cost_estimate=cost(2 * points_here * strain_rows * bins_here, 6_000_000),
         name="green",
-    )(
-        strain_green.reshape(points_here * strain_rows, bins_here),
-        green_scale.reshape(blocks_here, 1, strain_rows),
-        mechanism,
-    )
-
-    spectrum_shape = jax.ShapeDtypeStruct((4, variations, bins_here), f32)
-    spectra = pl.pallas_call(
-        functools.partial(spectra_kernel, blocks_here, samples),
-        out_shape=[spectrum_shape] * pt_size,
-        in_specs=[SMEM] * 3 + [VMEM] * (1 + pt_size),
-        out_specs=[VMEM] * pt_size,
-        scratch_shapes=[
-            pltpu.VMEM((4, variations * bins_here // 4, 2 * block_points), bf16),
-            pltpu.VMEM((4, variations, bins_here), f32),
-        ],
-        compiler_params=params(),
-        name="spectra",
-    )(rupture_row, rupture_blocks, block_count, green, *received)
-
-    gathered = [spectra[0]] + [swap(spectra[step], step) for step in range(1, pt_size)]
+    )(head, *in_hbm(strain_lines, green_scale, mechanism))
+
+    spectra = spectra_call(rupture_row, rupture_blocks, block_count, green, received)
+    gathered = exchange(spectra)
 
     table = fourier_table(bins, samples, samples_here)
     table_high, table_low = split_table(table)
@@ -344,7 +446,7 @@
         out_specs=VMEM,
         compiler_params=params(),
         name="excess",
-    )(band, *gathered)
+    )(band, *gathered[::-1])
     other = lax.ppermute(excess, "cmp", [(0, 1), (1, 0)])
 
     return pl.pallas_call(

time: 34.8 us -> 25.6 us (0.74)
  local copies, waits for them, and re-layouts: 7.25 us -> 0.03 us
  waiting for transfers between devices: 6.44 us -> 4.31 us
  Pallas kernels: 10.1 us -> 10.6 us
    unnamed x32 -> x14, local copies, waits for them, and re-layouts: 6.56 us -> 0.03 us
    ppermute x6, waiting for transfers between devices: 5.2 us -> 3.07 us  [swap(): return lax.ppermute(value, 'pt', [(i, i ^ step) for i in range(pt_size)])]
    pallas_call x1, Pallas kernels: 0.64 us -> 1.39 us  [body(): pl.pallas_call(functools.partial(pack_kernel, blocks_here, block_points),...]
    reshape x1 -> x0, local copies, waits for them, and re-layouts: 0.69 us -> none  [body(): green_scale.reshape(blocks_here, 1, strain_rows)]
    ppermute x6, starting transfers between devices: 10.4 us -> 10.1 us  [swap(): return lax.ppermute(value, 'pt', [(i, i ^ step) for i in range(pt_size)])]
  transfers between devices with their start and end apart: 7 -> 7, of which waited for: 3 -> 4; matrix products, arithmetic and copies ran while one was open for 2% -> 0% of each run, Pallas kernels for 14% -> 17%
where the time goes in v2:
time: 25.6 us; the launch traced here: 25.2 us
  Pallas kernels  10.6 us (41%)
  starting transfers between devices  10.2 us (40%)
  waiting for transfers between devices  4.31 us (17%)
    ppermute x6, starting transfers between devices, swap(): return lax.ppermute(value, 'pt', [(i, i ^ step) for i in range(pt_size)])  10.1 us
    pallas_call x1, Pallas kernels, body(): pl.pallas_call(green_kernel, out_shape=jax.ShapeDtypeStruct((blocks_here,...  4.15 us
    pallas_call x1, Pallas kernels, spectra_call(): pl.pallas_call(functools.partial(spectra_kernel, blocks_here, samples), o...  3.43 us
    ppermute x6, waiting for transfers between devices, swap(): return lax.ppermute(value, 'pt', [(i, i ^ step) for i in range(pt_size)])  3.07 us
    pallas_call x1, Pallas kernels, body(): pl.pallas_call(functools.partial(merge_kernel, bins, samples), out_shape=...  1.41 us
    pallas_call x1, Pallas kernels, body(): pl.pallas_call(functools.partial(pack_kernel, blocks_here, block_points),...  1.39 us
    ppermute x1, waiting for transfers between devices, body(): other = lax.ppermute(excess, 'cmp', [(0, 1), (1, 0)])  1.24 us
  transfers between devices with their start and end apart: 7, of which 4 were waited for; matrix products, arithmetic and copies ran while one was open for 0% of the time, Pallas kernels for 17%

profile of v2, /device:TPU:0, one launch (start us, length us, event | category | flops | bytes accessed | tf_op | source)
XLA Modules:
  0.0 25.2 jit_solution(2262896678773470693)
XLA Ops:
  0.0 1.4 %pack.1 = (bf16[5,3,16,128]{3,2,1,0:T(8,128)(2,1)S(1)}, bf16[5,3,16,128]{3,2,1,0:T(8,128)(2,1)S(1)}, bf16[5,3,16,128]{3,2,1,0:T(8,128)(2,1)S(1)}, bf16[5,3,16,12...) custom-call(s32[4]{0:T(128)} %row_ref.1, s32[4,12]{1,0:T(4,128)} %blocks_hbm.1, s32[4]{0:T(128)} %count_hbm.1, ...), custom_call_target="tpu_custom_call" | custom-call | tf_op jit(solution)/shard_map/pack/pallas_call | solution.py:382
  1.4 0.0 copy-start.2
  1.4 0.0 copy-start.3
  1.4 0.0 copy-start.4
  1.4 5.0 %collective-permute-start = (bf16[5,3,16,128]{3,2,1,0:T(8,128)(2,1)S(1)}, bf16[5,3,16,128]{3,2,1,0:T(8,128)(2,1)S(1)}, u32[]{:S(2)}, u32[]{:S(2)}) collective-permute-start(bf16[5,3,16,128]{3,2,1,0:T(8,128)(2,1)S(1)} %get-tuple-element.15), channel_id=1, source_target_pairs={{0,12},{4,8},{8,4},{12,0},{1,13},{5,9},{9,5},{13,1},{2,14},{6,10},... | collective-permute-start | bytes 184328 | tf_op jit(solution)/shard_map/ppermute | solution.py:399
  6.4 0.0 collective-permute-start.1
  6.4 0.6 %collective-permute-start.2 = (bf16[5,3,16,128]{3,2,1,0:T(8,128)(2,1)S(1)}, bf16[5,3,16,128]{3,2,1,0:T(8,128)(2,1)S(1)}, u32[]{:S(2)}, u32[]{:S(2)}) collective-permute-start(bf16[5,3,16,128]{3,2,1,0:T(8,128)(2,1)S(1)} %get-tuple-element.17), channel_id=1, source_target_pairs={{0,4},{4,0},{8,12},{12,8},{1,5},{5,1},{9,13},{13,9},{2,6},{6,2},{1... | collective-permute-start | bytes 184328 | tf_op jit(solution)/shard_map/ppermute | solution.py:399
  7.1 4.1 %green.1.green_ref = bf16[5,4,256,128]{3,2,1,0:T(8,128)(2,1)S(1)} custom-call(bf16[3072,128]{1,0:T(8,128)(2,1)S(1)} %get-tuple-element.14.head_ref, bf16[15360,128]{1,0:T(8,128)(2,1)} %bitcast.2, f32[5,24]{1,0:T(8,128)} %scale_hbm.1, f32[6,640]{1,0:T(8,128)} %mechanism_hbm.1), custom_call_target="tpu_custom_call" | custom-call | flops 3932160 | bytes 6000000 | tf_op jit(solution)/shard_map/green/pallas_call | solution.py:407
  11.2 0.0 collective-permute-done.refs_0_
  11.2 0.5 %collective-permute-done.1.refs_1_ = bf16[5,3,16,128]{3,2,1,0:T(8,128)(2,1)S(1)} collective-permute-done((bf16[5,3,16,128]{3,2,1,0:T(8,128)(2,1)S(1)}, bf16[5,3,16,128]{3,2,1,0:T(8,128)(2,1)S(1)}, u32[]{:S(2)}, u32[]{:S(2)}) %collective-permute-start.1) | collective-permute-done | bytes 61472 | tf_op jit(solution)/shard_map/ppermute | solution.py:399
  11.7 0.0 collective-permute-done.2.refs_2_
  11.7 3.4 %spectra.1 = (f32[4,16,128]{2,1,0:T(8,128)S(1)}, f32[4,16,128]{2,1,0:T(8,128)S(1)}, f32[4,16,128]{2,1,0:T(8,128)S(1)}, f32[4,16,128]{2,1,0:T(8,128)S(1)}) custom-call(s32[4]{0:T(128)} %row_ref.1, s32[4,12]{1,0:T(4,128)} %blocks_hbm.1, s32[4]{0:T(128)} %count_hbm.1, bf16[5,4,256,128]{3,2,1,0:T(8,128)(2,1)S(1)} %green.1.green_ref, ...), custom_call_target="tpu_custom_call" | custom-call | tf_op jit(solution)/shard_map/spectra/pallas_call | solution.py:287
  15.2 2.5 %collective-permute-start.3 = (f32[4,16,128]{2,1,0:T(8,128)S(1)}, f32[4,16,128]{2,1,0:T(8,128)S(1)}, u32[]{:S(2)}, u32[]{:S(2)}) collective-permute-start(f32[4,16,128]{2,1,0:T(8,128)S(1)} %get-tuple-element.19), channel_id=1, source_target_pairs={{0,12},{4,8},{8,4},{12,0},{1,13},{5,9},{9,5},{13,1},{2,14},{6,10},... | collective-permute-start | bytes 98312 | tf_op jit(solution)/shard_map/ppermute | solution.py:399
  17.6 0.2 collective-permute-start.4
  17.8 1.8 %collective-permute-start.5 = (f32[4,16,128]{2,1,0:T(8,128)S(1)}, f32[4,16,128]{2,1,0:T(8,128)S(1)}, u32[]{:S(2)}, u32[]{:S(2)}) collective-permute-start(f32[4,16,128]{2,1,0:T(8,128)S(1)} %get-tuple-element.21), channel_id=1, source_target_pairs={{0,4},{4,0},{8,12},{12,8},{1,5},{5,1},{9,13},{13,9},{2,6},{6,2},{1... | collective-permute-start | bytes 98312 | tf_op jit(solution)/shard_map/ppermute | solution.py:399
  19.6 0.0 copy-done.2
  19.6 0.0 copy-done.4
  19.6 0.2 band.1.band_ref
  19.9 1.1 %collective-permute-done.3.refs_0_ = f32[4,16,128]{2,1,0:T(8,128)S(1)} collective-permute-done((f32[4,16,128]{2,1,0:T(8,128)S(1)}, f32[4,16,128]{2,1,0:T(8,128)S(1)}, u32[]{:S(2)}, u32[]{:S(2)}) %collective-permute-start.3) | collective-permute-done | bytes 32800 | tf_op jit(solution)/shard_map/ppermute | solution.py:399
  21.0 1.5 %collective-permute-done.4.refs_1_ = f32[4,16,128]{2,1,0:T(8,128)S(1)} collective-permute-done((f32[4,16,128]{2,1,0:T(8,128)S(1)}, f32[4,16,128]{2,1,0:T(8,128)S(1)}, u32[]{:S(2)}, u32[]{:S(2)}) %collective-permute-start.4) | collective-permute-done | bytes 32800 | tf_op jit(solution)/shard_map/ppermute | solution.py:399
  22.5 0.0 collective-permute-done.5.refs_2_
  22.5 0.1 collective-permute-start.6
  22.6 1.2 %collective-permute-done.6.other_ref = f32[32,512]{1,0:T(8,128)S(1)} collective-permute-done((f32[32,512]{1,0:T(8,128)S(1)}, f32[32,512]{1,0:T(8,128)S(1)}, u32[]{:S(2)}, u32[]{:S(2)}) %collective-permute-start.6) | collective-permute-done | bytes 65568 | tf_op jit(solution)/shard_map/ppermute | solution.py:450
  23.8 1.4 %merge.1 = f32[1,16,2,256]{3,2,1,0:T(2,128)} custom-call(s32[4]{0:T(128)S(1)} %copy-done.5, s32[4]{0:T(128)S(1)} %copy-done.6, f32[32,512]{1,0:T(8,128)S(1)} %excess.1.own_ref, f32[32,512]{1,0:T(8,128)S(1)} %collective-permute-done.6.other_ref, f32[1,16,2,256]{3,2,1,0:T(2,128)S(1)} %copy-done.4, bf16[512,256]{1,0:T(8,128)(2,1)S(1)} %copy-done, ...), custom_call_target="tpu_custom_call" | custom-call | tf_op jit(solution)/shard_map/merge/pallas_call | solution.py:452
  (10 shorter events, 0.0 us)
Async XLA Ops:
  1.4 18.2 %copy-start.2 = (bf16[256,512]{1,0:T(8,128)(2,1)S(1)}, bf16[256,512]{1,0:T(8,128)(2,1)}, u32[]{:S(2)}) copy-start(bf16[256,512]{1,0:T(8,128)(2,1)} %constant.8.clone.table_high) | copy-start | bytes 786436
  1.4 18.2 %copy-start.3 = (bf16[256,512]{1,0:T(8,128)(2,1)S(1)}, bf16[256,512]{1,0:T(8,128)(2,1)}, u32[]{:S(2)}) copy-start(bf16[256,512]{1,0:T(8,128)(2,1)} %constant.9.clone.table_low) | copy-start | bytes 786436
  1.4 18.2 %copy-start.4 = (f32[1,16,2,256]{3,2,1,0:T(2,128)S(1)}, f32[1,16,2,256]{3,2,1,0:T(2,128)}, u32[]{:S(2)}) copy-start(f32[1,16,2,256]{3,2,1,0:T(2,128)} %high_ref.3) | copy-start | bytes 98308
  1.4 9.8 %collective-permute-start = (bf16[5,3,16,128]{3,2,1,0:T(8,128)(2,1)S(1)}, bf16[5,3,16,128]{3,2,1,0:T(8,128)(2,1)S(1)}, u32[]{:S(2)}, u32[]{:S(2)}) collective-permute-start(bf16[5,3,16,128]{3,2,1,0:T(8,128)(2,1)S(1)} %get-tuple-element.15), channel_id=1, source_target_pairs={{0,12},{4,8},{8,4},{12,0},{1,13},{5,9},{9,5},{13,1},{2,14},{6,10},... | collective-permute-start | bytes 184328 | tf_op jit(solution)/shard_map/ppermute | solution.py:399
  6.4 5.3 %collective-permute-start.1 = (bf16[5,3,16,128]{3,2,1,0:T(8,128)(2,1)S(1)}, bf16[5,3,16,128]{3,2,1,0:T(8,128)(2,1)S(1)}, u32[]{:S(2)}, u32[]{:S(2)}) collective-permute-start(bf16[5,3,16,128]{3,2,1,0:T(8,128)(2,1)S(1)} %get-tuple-element.16), channel_id=1, source_target_pairs={{0,8},{4,12},{8,0},{12,4},{1,9},{5,13},{9,1},{13,5},{2,10},{6,14},... | collective-permute-start | bytes 184328 | tf_op jit(solution)/shard_map/ppermute | solution.py:399
  6.4 5.3 %collective-permute-start.2 = (bf16[5,3,16,128]{3,2,1,0:T(8,128)(2,1)S(1)}, bf16[5,3,16,128]{3,2,1,0:T(8,128)(2,1)S(1)}, u32[]{:S(2)}, u32[]{:S(2)}) collective-permute-start(bf16[5,3,16,128]{3,2,1,0:T(8,128)(2,1)S(1)} %get-tuple-element.17), channel_id=1, source_target_pairs={{0,4},{4,0},{8,12},{12,8},{1,5},{5,1},{9,13},{13,9},{2,6},{6,2},{1... | collective-permute-start | bytes 184328 | tf_op jit(solution)/shard_map/ppermute | solution.py:399
  7.1 16.7 %copy-start = (bf16[512,256]{1,0:T(8,128)(2,1)S(1)}, bf16[512,256]{1,0:T(8,128)(2,1)}, u32[]{:S(2)}) copy-start(bf16[512,256]{1,0:T(8,128)(2,1)} %constant.10.clone.table_high) | copy-start | bytes 786436
  7.1 16.7 %copy-start.1 = (bf16[512,256]{1,0:T(8,128)(2,1)S(1)}, bf16[512,256]{1,0:T(8,128)(2,1)}, u32[]{:S(2)}) copy-start(bf16[512,256]{1,0:T(8,128)(2,1)} %constant.11.clone.table_low) | copy-start | bytes 786436
  7.1 16.7 %copy-start.5 = (s32[4]{0:T(128)S(1)}, s32[4]{0:T(128)}, u32[]{:S(2)}) copy-start(s32[4]{0:T(128)} %row_ref.1) | copy-start | bytes 52
  7.1 16.7 %copy-start.6 = (s32[4]{0:T(128)S(1)}, s32[4]{0:T(128)}, u32[]{:S(2)}) copy-start(s32[4]{0:T(128)} %crossover_ref.1) | copy-start | bytes 52
  15.2 5.8 %collective-permute-start.3 = (f32[4,16,128]{2,1,0:T(8,128)S(1)}, f32[4,16,128]{2,1,0:T(8,128)S(1)}, u32[]{:S(2)}, u32[]{:S(2)}) collective-permute-start(f32[4,16,128]{2,1,0:T(8,128)S(1)} %get-tuple-element.19), channel_id=1, source_target_pairs={{0,12},{4,8},{8,4},{12,0},{1,13},{5,9},{9,5},{13,1},{2,14},{6,10},... | collective-permute-start | bytes 98312 | tf_op jit(solution)/shard_map/ppermute | solution.py:399
  17.6 4.8 %collective-permute-start.4 = (f32[4,16,128]{2,1,0:T(8,128)S(1)}, f32[4,16,128]{2,1,0:T(8,128)S(1)}, u32[]{:S(2)}, u32[]{:S(2)}) collective-permute-start(f32[4,16,128]{2,1,0:T(8,128)S(1)} %get-tuple-element.20), channel_id=1, source_target_pairs={{0,8},{4,12},{8,0},{12,4},{1,9},{5,13},{9,1},{13,5},{2,10},{6,14},... | collective-permute-start | bytes 98312 | tf_op jit(solution)/shard_map/ppermute | solution.py:399
  17.8 4.6 %collective-permute-start.5 = (f32[4,16,128]{2,1,0:T(8,128)S(1)}, f32[4,16,128]{2,1,0:T(8,128)S(1)}, u32[]{:S(2)}, u32[]{:S(2)}) collective-permute-start(f32[4,16,128]{2,1,0:T(8,128)S(1)} %get-tuple-element.21), channel_id=1, source_target_pairs={{0,4},{4,0},{8,12},{12,8},{1,5},{5,1},{9,13},{13,9},{2,6},{6,2},{1... | collective-permute-start | bytes 98312 | tf_op jit(solution)/shard_map/ppermute | solution.py:399
  22.5 1.3 %collective-permute-start.6 = (f32[32,512]{1,0:T(8,128)S(1)}, f32[32,512]{1,0:T(8,128)S(1)}, u32[]{:S(2)}, u32[]{:S(2)}) collective-permute-start(f32[32,512]{1,0:T(8,128)S(1)} %excess.1.own_ref), channel_id=1, source_target_pairs={{0,1},{1,0},{2,3},{3,2},{4,5},{5,4},{6,7},{7,6},{8,9},{9,8},{10,11... | collective-permute-start | bytes 196616 | tf_op jit(solution)/shard_map/ppermute | solution.py:450
